TPU v7x, 32 devices: a whole 2x2x4 slice. The times are simulated.
32 devices in a mesh: pages: 8 (over z, x), query: 4 (over y, core).
Axes of the slice: x: 2, y: 2, z: 4, core: 2. Of those that a mesh axis runs over, the one named last changes fastest.
Arguments:
- queries: bfloat16 [8, 48, 32, 128], P('pages', 'query'), may hold values from -8 to 8
- pages: bfloat16 [128, 1024, 128], P('pages', 'query'), may hold values from -8 to 8
- cand_owner: int32 [8, 3], P('pages'), may hold values from 0 to 7, all different within a row
- cand_slot: int32 [8, 3], P('pages'), may hold values from 0 to 15
Outputs:
- losses: float32 [8, 48], P('pages', 'query')
- query_grad: float32 [8, 48, 32, 128], P('pages', 'query')
- page_grad: float32 [128, 1024, 128], P('pages', 'query')
Inputs may be any that keep to these rules, and one draw needn't show every extreme that they name: `cand_owner`: each row names 3 different owner indices, and every index is named by some row.
All inputs are finite; a program needn't handle non-finite values.
Results may differ from a plain program's by a relative error of at most 0.0024.
Values may be sent and summed in bfloat16 or wider, within the bound.
A program may use at most 64 MiB of HBM per device.

v0:
```python
import jax
import jax.numpy as jnp
from jax import lax
from jax.sharding import PartitionSpec as P

SHARPNESS = 10.0
INV_TEMP = 20.0
LOSS_SCALE = 256.0
EPSILON = 1e-06


def normalize(embeddings):
    values = embeddings.astype(jnp.float32)
    inverse = lax.rsqrt(jnp.sum(values * values, axis=-1, keepdims=True) + EPSILON)
    return (values * inverse, inverse)


def unnormalize_grad(unit_vectors, inverse, gradient):
    return inverse * (
        gradient - unit_vectors * jnp.sum(unit_vectors * gradient, axis=-1, keepdims=True)
    )


def coefficients(totals, tokens):
    candidates = totals.shape[0]
    queries_here = totals.shape[1] // tokens
    shaped = totals.reshape(candidates, queries_here, tokens)
    per_token = jnp.log(shaped) / SHARPNESS
    logits = INV_TEMP * jnp.mean(per_token, axis=2)
    exponentials = jnp.exp(logits)
    denominator = jnp.sum(exponentials, axis=0)
    losses = jnp.log(denominator) - logits[0]
    positive = (jnp.arange(candidates) == 0).astype(jnp.float32)[:, None]
    probability = exponentials / denominator
    scaled = LOSS_SCALE * INV_TEMP / tokens * (probability - positive)
    weights = scaled[:, :, None] / shaped
    return (weights.reshape(candidates, queries_here * tokens), losses)


def local(queries, pages, cand_owner, cand_slot):
    queries_local = queries.shape[1]
    tokens = queries.shape[2]
    embed_width = queries.shape[3]
    owners_count = lax.axis_size("pages")
    q_unit, q_inv = normalize(queries[0])
    q_round = q_unit.astype(jnp.bfloat16).reshape(queries_local * tokens, embed_width)
    query_rows = lax.all_gather(q_round, "query", axis=0, tiled=True)
    d_unit, d_inv = normalize(pages)
    d_round = d_unit.astype(jnp.bfloat16)
    owners = cand_owner[0]
    local_slots = cand_slot[0]
    owner_range = jnp.arange(owners_count, dtype=jnp.int32)
    wanted = jnp.sum(
        jnp.where(owners[None, :] == owner_range[:, None], local_slots[None, :], 0), axis=1
    )
    asked_slots = lax.all_to_all(wanted, "pages", split_axis=0, concat_axis=0, tiled=True)
    outgoing = jnp.take(d_round, asked_slots, axis=0)
    fetched = lax.all_to_all(outgoing, "pages", split_axis=0, concat_axis=0, tiled=True)
    chosen = jnp.take(fetched, owners, axis=0)

    def forward(unused, page_piece):
        scores = jnp.einsum("re,pe->rp", query_rows, page_piece, preferred_element_type=jnp.float32)
        return (unused, jnp.sum(jnp.exp(SHARPNESS * scores), axis=1))

    _, partial_value = lax.scan(forward, None, chosen)
    totals = lax.psum(partial_value, "query")
    weights, losses_all = coefficients(totals, tokens)
    losses = lax.dynamic_slice_in_dim(
        losses_all, lax.axis_index("query") * queries_local, queries_local
    )

    def shares_of(page_piece, weight_row):
        scores = jnp.einsum("re,pe->rp", query_rows, page_piece, preferred_element_type=jnp.float32)
        return (weight_row[:, None] * jnp.exp(SHARPNESS * scores)).astype(jnp.bfloat16)

    start_rows = jnp.zeros((query_rows.shape[0], embed_width), jnp.float32)

    def page_side(unused, pair):
        page_piece, weight_row = pair
        shares = shares_of(page_piece, weight_row)
        return (
            unused,
            jnp.einsum("rp,re->pe", shares, query_rows, preferred_element_type=jnp.float32),
        )

    def query_side(grad_rows, pair):
        page_piece, weight_row = pair
        shares = shares_of(page_piece, weight_row)
        return (grad_rows + jnp.dot(shares, page_piece, preferred_element_type=jnp.float32), None)

    _, page_terms = lax.scan(page_side, None, (chosen, weights))
    grad_rows, _ = lax.scan(query_side, start_rows, (chosen, weights))
    candidates = owners.shape[0]
    selector = (owner_range[:, None] == owners[None, :]).astype(jnp.float32)
    returning = jnp.dot(
        selector, page_terms.reshape(candidates, -1), precision=lax.Precision.HIGHEST
    )
    returning = returning.reshape(owners_count, page_terms.shape[1], embed_width)
    returned = lax.all_to_all(returning, "pages", split_axis=0, concat_axis=0, tiled=True)
    own_grads = lax.psum_scatter(grad_rows, "query", scatter_dimension=0, tiled=True)
    query_grad = unnormalize_grad(
        q_unit, q_inv, own_grads.reshape(queries_local, tokens, embed_width)
    )
    page_range = jnp.arange(pages.shape[0], dtype=jnp.int32)
    picker = (page_range[:, None] == asked_slots[None, :]).astype(jnp.float32)
    summed = jnp.dot(picker, returned.reshape(owners_count, -1), precision=lax.Precision.HIGHEST)
    summed = summed.reshape(pages.shape[0], pages.shape[1], embed_width)
    page_grad = unnormalize_grad(d_unit, d_inv, summed)
    return (losses[None, :], query_grad[None], page_grad)


def solution(mesh):
    return jax.shard_map(
        local,
        mesh=mesh,
        in_specs=(
            P("pages", "query", None, None),
            P("pages", "query", None),
            P("pages", None),
            P("pages", None),
        ),
        out_specs=(P("pages", "query"), P("pages", "query", None, None), P("pages", "query", None)),
        check_vma=False,
    )
```

profile of v0, /device:TPU:0, one launch (start us, length us, event | category | flops | bytes accessed | tf_op | source)
XLA Modules:
  0.0 144.6 jit_solution(10739573871857995714)
XLA Ops:
  8.7 7.3 %all-to-all-start = ((s32[8,1,1]{2,1,0:T(1,128)}), s32[8,1,1]{2,1,0:T(1,128)S(1)}, u32[]{:S(2)}, u32[]{:S(2)}) async-start(s32[8,1,1]{2,1,0:T(1,128)} %copy.20), calls=%async_computation | async-start | bytes 8192 | tf_op jit(solution)/shard_map/all_to_all | solution.py:56
  16.0 1.0 multiply_reduce_fusion.1
  17.1 1.9 %fusion.38 = f32[16,256]{0,1:T(8,128)S(1)} fusion(bf16[16,256,128]{2,1,0:T(8,128)(2,1)} %param.11), kind=kLoop, calls=%fused_computation.42 | loop fusion | flops 1568768 | bytes 1064960 | tf_op jit(solution)/shard_map/reduce_sum | solution.py:14
  19.1 2.9 %fusion.35 = bf16[16,256,128]{2,0,1:T(8,128)(2,1)S(1)} fusion(f32[16,256]{0,1:T(8,128)S(1)} %add_rsqrt_fusion, bf16[16,256,128]{2,1,0:T(8,128)(2,1)S(1)} %copy-done), kind=kLoop, calls=%fused_computation.39 | loop fusion | flops 1572864 | bytes 2113536 | tf_op jit(solution)/shard_map/convert_element_type | solution.py:49
  23.3 0.9 broadcast_select_fusion
  24.2 5.9 %all-to-all-start.1 = ((bf16[8,256,128]{2,1,0:T(8,128)(2,1)}), bf16[8,256,128]{2,1,0:T(8,128)(2,1)S(1)}, u32[]{:S(2)}, u32[]{:S(2)}) async-start(bf16[8,256,128]{2,1,0:T(8,128)(2,1)} %broadcast_select_fusion), calls=%async_computation.1 | async-start | bytes 1048576 | tf_op jit(solution)/shard_map/all_to_all | solution.py:58
  30.3 6.5 %all_gather.3 = bf16[1536,128]{1,0:T(8,128)(2,1)S(1)} all-gather(bf16[384,128]{1,0:T(8,128)(2,1)S(1)} %fusion.47), channel_id=1, replica_groups=mesh['pages'=8,'query'=4] {'query'}, dimensions={0}, use_global_device_ids=true | all-gather | bytes 491520 | tf_op jit(solution)/shard_map/all_gather | solution.py:47
  36.8 7.3 %all-to-all-done.1 = bf16[8,256,128]{2,1,0:T(8,128)(2,1)S(1)} async-done(((bf16[8,256,128]{2,1,0:T(8,128)(2,1)}), bf16[8,256,128]{2,1,0:T(8,128)(2,1)S(1)}, u32[]{:S(2)}, u32[]{:S(2)}) %all-to-all-start.1) | async-done | bytes 524320 | tf_op jit(solution)/shard_map/all_to_all | solution.py:58
  44.7 1.6 %while.31 = (s32[]{:T(128)}, f32[3,1536]{1,0:T(4,128)S(1)}, bf16[3,256,128]{2,1,0:T(8,128)(2,1)S(1)}, bf16[1536,128]{1,0:T(8,128)(2,1)S(1)}, s32[]{:T(128)}, /*index=5*/s32[]{:T(128)}) while((s32[]{:T(128)}, f32[3,1536]{1,0:T(4,128)S(1)}, bf16[3,256,128]{2,1,0:T(8,128)(2,1)S(1)}, bf16[1536,128]{1,0:T(8,128)(2,1)S(1)}, s32[]{:T(128)}, ...), condition=%wide.region_5.6_spmd, body=%wide.region_3.5_spmd.sunk | while | flops 101448192 | bytes 489557 | solution.py:65
  46.3 10.3 %psum.7 = f32[3,1536]{1,0:T(4,128)S(1)} all-reduce(f32[3,1536]{1,0:T(4,128)S(1)} %get-tuple-element.79), channel_id=1, replica_groups=mesh['pages'=8,'query'=4] {'query'}, use_global_device_ids=true, to_apply=%region_6.7 | all-reduce | flops 4608 | bytes 36864 | tf_op jit(solution)/shard_map/psum | solution.py:66
  57.2 2.0 %while.32 = (s32[]{:T(128)}, f32[3,256,128]{2,1,0:T(8,128)S(1)}, f32[3,1536]{1,0:T(4,128)S(1)}, bf16[3,256,128]{2,1,0:T(8,128)(2,1)S(1)}, bf16[1536,128]{1,0:T(8,128)(2,1)S(1)}, /*index=5*/s32[]{:T(128)}) while((s32[]{:T(128)}, f32[3,256,128]{2,1,0:T(8,128)S(1)}, f32[3,1536]{1,0:T(4,128)S(1)}, bf16[3,256,128]{2,1,0:T(8,128)(2,1)S(1)}, ...), condition=%wide.region_14.15_spmd, body=%wide.region_13.14_spmd.sunk | while | flops 202506240 | bytes 1004625 | solution.py:91
  59.1 2.9 %while.33 = (s32[]{:T(128)}, f32[1536,128]{1,0:T(8,128)S(1)}, f32[3,1536]{1,0:T(4,128)S(1)}, bf16[3,256,128]{2,1,0:T(8,128)(2,1)S(1)}, bf16[1536,128]{1,0:T(8,128)(2,1)S(1)}, /*index=5*/s32[]{:T(128)}, s32[]{:T(128)}) while((s32[]{:T(128)}, f32[1536,128]{1,0:T(8,128)S(1)}, f32[3,1536]{1,0:T(4,128)S(1)}, ...), condition=%wide.region_10.11_spmd.clone, body=%wide.region_9.10_spmd.clone.sunk | while | flops 202899456 | bytes 2119266 | solution.py:92
  60.1 0.9 convolution_add_fusion.2
  61.1 0.9 convolution_add_fusion.2
  62.9 0.9 fusion.45
  63.8 1.2 copy.23
  65.0 4.1 %all-to-all-start.2 = ((f32[8,256,128]{2,1,0:T(8,128)}), f32[8,256,128]{2,1,0:T(8,128)S(1)}, u32[]{:S(2)}, u32[]{:S(2)}) async-start(f32[8,256,128]{2,1,0:T(8,128)} %copy.23), calls=%async_computation.3 | async-start | bytes 2097152 | tf_op jit(solution)/shard_map/all_to_all | solution.py:99
  69.7 15.8 %reduce-scatter.2.cloned.1.call-done = f32[384,128]{1,0:T(8,128)} async-done(((f32[1536,128]{1,0:T(8,128)}), f32[384,128]{1,0:T(8,128)}) %reduce-scatter.2.cloned.1.call-update) | async-done | bytes 196624 | tf_op jit(solution)/shard_map/reduce_scatter | solution.py:100
  85.5 1.1 multiply_reduce_fusion
  86.7 1.8 %subtract_multiply_fusion = f32[1,12,32,128]{3,2,1,0:T(8,128)} fusion(f32[1,12,32,128]{3,2,1,0:T(8,128)} %bitcast.85, bf16[1,12,32,128]{3,2,1,0:T(8,128)(2,1)S(1)} %copy-done.1, f32[12,32]{1,0:T(8,128)S(1)} %mul.140, f32[12,32]{1,0:T(8,128)S(1)} %add_rsqrt_fusion.1), kind=kLoop, calls=%fused_computation.54 | loop fusion | flops 245760 | bytes 494592 | tf_op jit(solution)/shard_map/mul | solution.py:19
  88.5 6.3 %all-to-all-done.2 = f32[8,256,128]{2,1,0:T(8,128)S(1)} async-done(((f32[8,256,128]{2,1,0:T(8,128)}), f32[8,256,128]{2,1,0:T(8,128)S(1)}, u32[]{:S(2)}, u32[]{:S(2)}) %all-to-all-start.2) | async-done | bytes 1048608 | tf_op jit(solution)/shard_map/all_to_all | solution.py:99
  94.8 1.5 %fusion.41 = f32[16,256,128]{2,0,1:T(8,128)S(1)} fusion(f32[1,8,256,128]{3,2,1,0:T(8,128)S(1)} %bitcast.84, s32[8]{0:T(128)S(1)} %reduce.5), kind=kOutput, calls=%fused_computation.45 | convolution fusion | flops 50331776 | bytes 3145760 | tf_op jit(solution)/shard_map/dot_general | solution.py:106
  96.3 39.4 %fusion.37 = f32[16,256,128]{2,0,1:T(8,128)S(1)} fusion(f32[16,256,128]{2,0,1:T(8,128)S(1)} %fusion.41, f32[16,256]{0,1:T(8,128)S(1)} %add_rsqrt_fusion, bf16[16,256,128]{2,1,0:T(8,128)(2,1)S(1)} %copy-done), kind=kOutput, calls=%fused_computation.41 | output fusion | flops 4198527 | bytes 5259264 | tf_op jit(solution)/shard_map/mul | solution.py:20
  135.8 2.0 %copy.24 = f32[16,256,128]{2,1,0:T(8,128)} copy(f32[16,256,128]{2,0,1:T(8,128)S(1)} %fusion.37) | data formatting | bytes 4194304
  (64 shorter events, 10.1 us)
Async XLA Ops:
  7.2 11.9 %copy-start = (bf16[16,256,128]{2,1,0:T(8,128)(2,1)S(1)}, bf16[16,256,128]{2,1,0:T(8,128)(2,1)}, u32[]{:S(2)}) copy-start(bf16[16,256,128]{2,1,0:T(8,128)(2,1)} %param.11) | copy-start | bytes 3145732
  8.7 13.6 %all-to-all-start = ((s32[8,1,1]{2,1,0:T(1,128)}), s32[8,1,1]{2,1,0:T(1,128)S(1)}, u32[]{:S(2)}, u32[]{:S(2)}) async-start(s32[8,1,1]{2,1,0:T(1,128)} %copy.20), calls=%async_computation | async-start | bytes 8192 | tf_op jit(solution)/shard_map/all_to_all | solution.py:56
  22.2 7.9 %copy-start.4 = (s32[1,3]{1,0:T(1,128)S(1)}, s32[1,3]{1,0:T(1,128)}, u32[]{:S(2)}) copy-start(s32[1,3]{1,0:T(1,128)} %param.12) | copy-start | bytes 40
  22.2 7.9 %copy-start.1 = (bf16[1,12,32,128]{3,2,1,0:T(8,128)(2,1)S(1)}, bf16[1,12,32,128]{3,2,1,0:T(8,128)(2,1)}, u32[]{:S(2)}) copy-start(bf16[1,12,32,128]{3,2,1,0:T(8,128)(2,1)} %param.10) | copy-start | bytes 294916
  24.2 19.9 %all-to-all-start.1 = ((bf16[8,256,128]{2,1,0:T(8,128)(2,1)}), bf16[8,256,128]{2,1,0:T(8,128)(2,1)S(1)}, u32[]{:S(2)}, u32[]{:S(2)}) async-start(bf16[8,256,128]{2,1,0:T(8,128)(2,1)} %broadcast_select_fusion), calls=%async_computation.1 | async-start | bytes 1048576 | tf_op jit(solution)/shard_map/all_to_all | solution.py:58
  30.1 55.4 %reduce-scatter.2.cloned.1.call-start = ((), (), s32[]{:S(2)}) async-start(), calls=%async_computation.4 | async-start | bytes 983040 | tf_op jit(solution)/shard_map/reduce_scatter | solution.py:100
  57.1 2.0 %copy-start.2 = (f32[1536,128]{1,0:T(8,128)S(1)}, f32[1536,128]{1,0:T(8,128)}, u32[]{:S(2)}) copy-start(f32[1536,128]{1,0:T(8,128)} %custom-call) | copy-start | bytes 2359300
  62.0 0.9 copy-start.3
  65.0 29.8 %all-to-all-start.2 = ((f32[8,256,128]{2,1,0:T(8,128)}), f32[8,256,128]{2,1,0:T(8,128)S(1)}, u32[]{:S(2)}, u32[]{:S(2)}) async-start(f32[8,256,128]{2,1,0:T(8,128)} %copy.23), calls=%async_computation.3 | async-start | bytes 2097152 | tf_op jit(solution)/shard_map/all_to_all | solution.py:99
Sparse Core Ops, SparseCore 0:
  63.0 22.4 reduce-scatter.1
where the time goes:
time: 145 us
  other arithmetic  50.6 us (35%)
  waiting for transfers between devices  29.4 us (20%)
  starting transfers between devices  17.3 us (12%)
  blocking collectives  16.8 us (12%)
  between operations  14.3 us (10%)
  matrix products  8.08 us (6%)
  local copies, waits for them, and re-layouts  7.7 us (5%)
    mul x1, other arithmetic, unnormalize_grad(): unit_vectors * jnp.sum(unit_vectors * gradient, axis=-1, keepdims=True)  39.4 us
    reduce_scatter x1, waiting for transfers between devices, local(): lax.psum_scatter(grad_rows, 'query', scatter_dimension=0, tiled=True)  15.8 us
    psum x1, blocking collectives, local(): totals = lax.psum(partial_value, 'query')  10.3 us
    all_to_all x1, waiting for transfers between devices, local(): lax.all_to_all(outgoing, 'pages', split_axis=0, concat_axis=0, tiled=True)  7.26 us
    all_to_all x1, starting transfers between devices, local(): lax.all_to_all(wanted, 'pages', split_axis=0, concat_axis=0, tiled=True)  7.25 us
    all_gather x1, blocking collectives, local(): query_rows = lax.all_gather(q_round, 'query', axis=0, tiled=True)  6.49 us
    all_to_all x1, waiting for transfers between devices, local(): lax.all_to_all(returning, 'pages', split_axis=0, concat_axis=0, tiled=True)  6.3 us
    all_to_all x1, starting transfers between devices, local(): lax.all_to_all(outgoing, 'pages', split_axis=0, concat_axis=0, tiled=True)  5.91 us
  transfers between devices with their start and end apart: 4, of which 4 were waited for; matrix products, arithmetic and copies ran while one was open for 8% of the time, Pallas kernels for 0%

commit v1 on v0

v1 whole, which is shorter than its diff:
```python
import functools
import math

import jax
import jax.numpy as jnp
from jax import lax
from jax.experimental import pallas as pl
from jax.experimental.pallas import tpu as pltpu
from jax.sharding import PartitionSpec as P

SHARPNESS = 10.0
INV_TEMP = 20.0
LOSS_SCALE = 256.0
EPSILON = 1e-06
LANES = 128
MESH = pl.DeviceIdType.MESH
VMEM_BYTES = 56 * 2**20
F32 = jnp.float32
BF16 = jnp.bfloat16


def normalize(embeddings):
    values = embeddings.astype(F32)
    inverse = lax.rsqrt(jnp.sum(values * values, axis=-1, keepdims=True) + EPSILON)
    return values * inverse, inverse


def unnormalize_grad(unit_vectors, inverse, gradient):
    return inverse * (
        gradient - unit_vectors * jnp.sum(unit_vectors * gradient, axis=-1, keepdims=True)
    )


def group_sums(values, size):
    width = values.shape[1]
    lane = lax.broadcasted_iota(jnp.int32, values.shape, 1)
    step = 1
    while step < size:
        upper = (lane & step) != 0
        values = values + jnp.where(
            upper, pltpu.roll(values, step, 1), pltpu.roll(values, width - step, 1)
        )
        step *= 2
    return values


def exchange_kernel(
    owners, groups, candidates, tokens,
    q_ref, pages_ref, owner_ref, slot_ref,
    loss_ref, qgrad_ref, back_ref, asked_ref,
    q_all, d_round, asked, asked_smem, send, fetched, turned, sums, rows_ref, weight_ref,
    shares, terms, q_part, q_got,
    ask_out, ask_in, page_out, page_in, back_out, back_in,
    q_out, q_in, sum_out, sum_in, part_out, part_in, local_sem,
):
    me = lax.axis_index("pages")
    mine = lax.axis_index("query")
    page_count = pages_ref.shape[0]
    rows = q_ref.shape[0]
    padded = rows_ref.shape[0]

    def to_owner(k):
        return lax.rem(me + k, owners)

    def from_owner(k):
        return lax.rem(me + owners - k, owners)

    def to_group(k):
        return lax.rem(mine + k, groups)

    def from_group(k):
        return lax.rem(mine + groups - k, groups)

    def across_pages(src, dst, out, into, k):
        return pltpu.make_async_remote_copy(
            src_ref=src, dst_ref=dst, send_sem=out.at[k], recv_sem=into.at[k],
            device_id=(to_owner(k), mine), device_id_type=MESH,
        )

    def across_query(src, dst, out, into, k):
        return pltpu.make_async_remote_copy(
            src_ref=src, dst_ref=dst, send_sem=out.at[k], recv_sem=into.at[k],
            device_id=(me, to_group(k)), device_id_type=MESH,
        )

    def each(count, body):
        lax.fori_loop(1, count, lambda k, c: (body(k), c)[1], 0)

    barrier = pltpu.get_barrier_semaphore()
    each(owners, lambda k: pl.semaphore_signal(
        barrier, inc=1, device_id=(to_owner(k), mine), device_id_type=MESH))
    each(groups, lambda k: pl.semaphore_signal(
        barrier, inc=1, device_id=(me, to_group(k)), device_id_type=MESH))

    lane = lax.broadcasted_iota(jnp.int32, (1, LANES), 1)
    wanted = jnp.full((1, LANES), -1, jnp.int32)
    for c in range(candidates):
        wanted = jnp.where(lane == owner_ref[0, c], slot_ref[0, c], wanted)
    asked[me] = wanted
    q_unit, q_inv = normalize(q_ref[...])
    q_all[mine] = q_unit.astype(BF16)
    pl.semaphore_wait(barrier, owners + groups - 2)

    each(owners, lambda k: across_pages(asked.at[me], asked.at[me], ask_out, ask_in, k).start())
    each(groups, lambda k: across_query(q_all.at[mine], q_all.at[mine], q_out, q_in, k).start())

    def round_page(j, carry):
        d_round[j] = normalize(pages_ref[j])[0].astype(BF16)
        return carry

    lax.fori_loop(0, page_count, round_page, 0)

    def ask_arrived(k):
        across_pages(asked.at[from_owner(k)], asked.at[from_owner(k)], ask_out, ask_in, k).wait_recv()
        across_pages(asked.at[me], asked.at[me], ask_out, ask_in, k).wait_send()

    each(owners, ask_arrived)
    to_scalars = pltpu.make_async_copy(asked, asked_smem, local_sem)
    to_scalars.start()
    asked_ref[...] = asked[...]
    to_scalars.wait()

    def serve(k):
        to = to_owner(k)
        send[k] = d_round[jnp.maximum(asked_smem[to, 0, me], 0)]
        across_pages(send.at[k], fetched.at[me], page_out, page_in, k).start()

    each(owners, serve)
    fetched[me] = d_round[jnp.maximum(asked_smem[me, 0, me], 0)]

    def query_arrived(k):
        across_query(q_all.at[from_group(k)], q_all.at[from_group(k)], q_out, q_in, k).wait_recv()
        across_query(q_all.at[mine], q_all.at[mine], q_out, q_in, k).wait_send()

    each(groups, query_arrived)

    def page_arrived(k):
        across_pages(send.at[k], fetched.at[from_owner(k)], page_out, page_in, k).wait()

    each(owners, page_arrived)

    def exponentials(page, g):
        scores = lax.dot_general(
            page, q_all[g], (((1,), (1,)), ((), ())), preferred_element_type=F32
        )
        return jnp.exp2(scores * (SHARPNESS * math.log2(math.e)))

    def forward(c, carry):
        page = fetched[owner_ref[0, c]]
        turned[c] = page.T
        for g in range(groups):
            sums[mine, c, :, g * rows : (g + 1) * rows] = jnp.sum(
                exponentials(page, g), axis=0, keepdims=True
            )
        return carry

    lax.fori_loop(0, candidates, forward, 0)
    each(groups, lambda k: across_query(sums.at[mine], sums.at[mine], sum_out, sum_in, k).start())

    def sums_arrived(k):
        across_query(sums.at[from_group(k)], sums.at[from_group(k)], sum_out, sum_in, k).wait_recv()
        across_query(sums.at[mine], sums.at[mine], sum_out, sum_in, k).wait_send()

    each(groups, sums_arrived)

    rows_ref[...] = jnp.ones_like(rows_ref)
    for c in range(candidates):
        total = sums[0, c]
        for g in range(1, groups):
            total = total + sums[g, c]
        rows_ref[c : c + 1, :] = total
    totals = rows_ref[...]
    logits = (INV_TEMP / SHARPNESS / tokens) * group_sums(jnp.log(totals), tokens)
    which = lax.broadcasted_iota(jnp.int32, totals.shape, 0)
    powers = jnp.where(which < candidates, jnp.exp(logits), 0.0)
    denominator = jnp.sum(powers, axis=0, keepdims=True)
    losses = jnp.log(denominator) - logits[0:1]
    positive = jnp.where(which == 0, 1.0, 0.0)
    weights = (LOSS_SCALE * INV_TEMP / tokens) * (powers / denominator - positive) / totals
    for g in range(groups):
        loss_ref[g] = losses[:, g * rows : (g + 1) * rows]
    for c in range(candidates):
        weight_ref[c] = weights[c : c + 1]

    def backward(c, carry):
        page = fetched[owner_ref[0, c]]
        term = jnp.zeros(page.shape, F32)
        for g in range(groups):
            share = (
                weight_ref[c, :, g * rows : (g + 1) * rows] * exponentials(page, g)
            ).astype(BF16)
            shares[c, g] = share
            term = term + jnp.dot(share, q_all[g], preferred_element_type=F32)
        terms[c] = term.astype(BF16)
        return carry

    lax.fori_loop(0, candidates, backward, 0)

    def term_for(owner):
        place = jnp.int32(0)
        for c in range(candidates):
            place = jnp.where(owner_ref[0, c] == owner, c, place)
        return terms[place]

    def give_back(k):
        send[k] = term_for(to_owner(k))
        across_pages(send.at[k], back_ref.at[me], back_out, back_in, k).start()

    each(owners, give_back)
    back_ref[me] = term_for(me)

    for k in range(1, groups + 1):
        g = to_group(k)

        def query_side(c, total, g=g):
            return total + jnp.dot(turned[c], shares[c, g], preferred_element_type=F32)

        q_part[k - 1] = lax.fori_loop(
            0, candidates, query_side, jnp.zeros(q_part.shape[1:], F32)
        )
        if k < groups:
            across_query(q_part.at[k - 1], q_got.at[k - 1], part_out, part_in, k).start()

    total = q_part[groups - 1]
    for k in range(1, groups):
        across_query(q_part.at[k - 1], q_got.at[k - 1], part_out, part_in, k).wait()
        total = total + q_got[k - 1]
    q_unit, q_inv = normalize(q_ref[...])
    qgrad_ref[...] = unnormalize_grad(q_unit, q_inv, total.T)

    def back_arrived(k):
        across_pages(send.at[k], back_ref.at[from_owner(k)], back_out, back_in, k).wait()

    each(owners, back_arrived)


def page_kernel(owners, asked_ref, pages_ref, back_ref, out_ref, total):
    me = lax.axis_index("pages")
    here = pages_ref.shape[0]
    for i in range(here):
        page = pl.program_id(0) * here + i

        def count(r, found):
            return found + jnp.where(asked_ref[r, me] == page, 1, 0)

        found = lax.fori_loop(0, owners, count, jnp.int32(0))

        @pl.when(found == 0)
        def _():
            out_ref[i] = jnp.zeros(out_ref.shape[1:], F32)

        @pl.when(found > 0)
        def _():
            total[...] = jnp.zeros_like(total)

            def add(r, carry):
                @pl.when(asked_ref[r, me] == page)
                def _():
                    total[...] += back_ref[r].astype(F32)

                return carry

            lax.fori_loop(0, owners, add, 0)
            d_unit, d_inv = normalize(pages_ref[i])
            out_ref[i] = unnormalize_grad(d_unit, d_inv, total[...])


def local(queries, pages, cand_owner, cand_slot):
    _, queries_local, tokens, width = queries.shape
    page_count, patches, _ = pages.shape
    owners = lax.axis_size("pages")
    groups = lax.axis_size("query")
    candidates = cand_owner.shape[1]
    rows = queries_local * tokens
    everyone = groups * rows
    padded = -(-candidates // 8) * 8
    dma = pltpu.SemaphoreType.DMA
    vmem = pl.BlockSpec(memory_space=pltpu.VMEM)
    smem = pl.BlockSpec(memory_space=pltpu.SMEM)
    losses, query_grad, back, asked = pl.pallas_call(
        functools.partial(exchange_kernel, owners, groups, candidates, tokens),
        out_shape=(
            jax.ShapeDtypeStruct((groups, 1, rows), F32),
            jax.ShapeDtypeStruct((rows, width), F32),
            jax.ShapeDtypeStruct((owners, patches, width), BF16),
            jax.ShapeDtypeStruct((owners, 1, LANES), jnp.int32),
        ),
        in_specs=[vmem, vmem, smem, smem],
        out_specs=(vmem, vmem, vmem, vmem),
        scratch_shapes=[
            pltpu.VMEM((groups, rows, width), BF16),
            pltpu.VMEM((page_count, patches, width), BF16),
            pltpu.VMEM((owners, 1, LANES), jnp.int32),
            pltpu.SMEM((owners, 1, LANES), jnp.int32),
            pltpu.VMEM((owners, patches, width), BF16),
            pltpu.VMEM((owners, patches, width), BF16),
            pltpu.VMEM((candidates, width, patches), BF16),
            pltpu.VMEM((groups, candidates, 1, everyone), F32),
            pltpu.VMEM((padded, everyone), F32),
            pltpu.VMEM((candidates, 1, everyone), F32),
            pltpu.VMEM((candidates, groups, patches, rows), BF16),
            pltpu.VMEM((candidates, patches, width), BF16),
            pltpu.VMEM((groups, width, rows), F32),
            pltpu.VMEM((groups, width, rows), F32),
        ]
        + [dma((owners,))] * 6
        + [dma((groups,))] * 6
        + [dma],
        compiler_params=pltpu.CompilerParams(
            collective_id=0, has_side_effects=True, vmem_limit_bytes=VMEM_BYTES
        ),
    )(queries.reshape(rows, width), pages, cand_owner, cand_slot)

    block = max(1, page_count // 4)
    whole = pl.BlockSpec((owners, patches, width), lambda i, asked: (0, 0, 0))
    some = pl.BlockSpec((block, patches, width), lambda i, asked: (i, 0, 0))
    page_grad = pl.pallas_call(
        functools.partial(page_kernel, owners),
        out_shape=jax.ShapeDtypeStruct((page_count, patches, width), F32),
        grid_spec=pltpu.PrefetchScalarGridSpec(
            num_scalar_prefetch=1,
            grid=(page_count // block,),
            in_specs=[some, whole],
            out_specs=some,
            scratch_shapes=[pltpu.VMEM((patches, width), F32)],
        ),
        compiler_params=pltpu.CompilerParams(vmem_limit_bytes=VMEM_BYTES),
    )(asked.reshape(owners, LANES), pages, back)
    own = lax.dynamic_index_in_dim(losses, lax.axis_index("query"), 0, keepdims=False)
    return (
        own.reshape(queries_local, tokens)[:, 0][None],
        query_grad.reshape(1, queries_local, tokens, width),
        page_grad,
    )


def solution(mesh):
    return jax.shard_map(
        local,
        mesh=mesh,
        in_specs=(
            P("pages", "query", None, None),
            P("pages", "query", None),
            P("pages", None),
            P("pages", None),
        ),
        out_specs=(P("pages", "query"), P("pages", "query", None, None), P("pages", "query", None)),
        check_vma=False,
    )
```

time: 145 us -> 50.8 us (0.35)
  the two profiles are of different devices: /device:TPU:0 before, /device:TPU:26 now
where the time goes in v1:
time: 50.8 us; the launch traced here: 50.5 us
  Pallas kernels  47.8 us (94%)
  local copies, waits for them, and re-layouts  2.09 us (4%)
  between operations  0.65 us (1%)
    pallas_call x1, Pallas kernels, local(): pl.pallas_call(functools.partial(exchange_kernel, owners, groups, candida...  42.3 us
    pallas_call x1, Pallas kernels, local(): pl.pallas_call(functools.partial(page_kernel, owners), out_shape=jax.Shap...  5.51 us

profile of v1, /device:TPU:26, one launch (start us, length us, event | category | flops | bytes accessed | tf_op | source)
XLA Modules:
  0.0 50.5 jit_solution(3107668607097302424)
XLA Ops:
  0.6 42.3 %shard_map.67 = (f32[4,1,384]{2,1,0:T(1,128)}, f32[384,128]{1,0:T(8,128)}, bf16[8,256,128]{2,1,0:T(8,128)(2,1)}, s32[8,1,128]{2,1,0:T(1,128)}) custom-call(bf16[384,128]{1,0:T(8,128)(2,1)} %bitcast.5, bf16[16,256,128]{2,1,0:T(8,128)(2,1)} %pages_ref.3, s32[1,3]{1,0:T(1,128)} %owner_ref.1, s32[1,3]{1,0:T(1,128)} %slot_ref.1), custom_call_target="tpu_custom_call" | custom-call | tf_op jit(solution)/shard_map/pallas_call | solution.py:280
  42.9 0.0 copy-start
  42.9 0.7 %dynamic-slice_reduce_fusion = f32[384]{0:T(512)S(1)} fusion(f32[4,1,384]{2,1,0:T(1,128)} %get-tuple-element.7, s32[]{:T(128)S(6)} %select_n.4), kind=kLoop, calls=%fused_computation.1 | loop fusion | bytes 3076 | tf_op jit(solution)/shard_map/jit(dynamic_index_in_dim)/dynamic_slice | solution.py:329
  43.6 0.1 reshape.20
  43.7 0.6 %slice_reduce_fusion = f32[12]{0:T(128)} fusion(f32[12,32]{1,0:T(8,128)S(1)} %reshape.20), kind=kLoop, calls=%fused_computation | loop fusion | bytes 96 | tf_op jit(solution)/shard_map/slice | solution.py:331
  44.3 5.5 %shard_map.68 = f32[16,256,128]{2,1,0:T(8,128)} custom-call(s32[8,128]{1,0:T(8,128)} %bitcast.6, bf16[16,256,128]{2,1,0:T(8,128)(2,1)} %pages_ref.3, bf16[8,256,128]{2,1,0:T(8,128)(2,1)} %get-tuple-element.10.back_ref), custom_call_target="tpu_custom_call" | custom-call | tf_op jit(solution)/shard_map/pallas_call | solution.py:317
  49.8 0.0 copy-done
  49.8 0.7 %copy.8 = f32[1,12,32,128]{3,2,1,0:T(8,128)} copy(f32[1,12,32,128]{3,2,1,0:T(8,128)S(1)} %bitcast.4) | data formatting | bytes 393216
Async XLA Ops:
  42.9 6.9 %copy-start = (f32[384,128]{1,0:T(8,128)S(1)}, f32[384,128]{1,0:T(8,128)}, u32[]{:S(2)}) copy-start(f32[384,128]{1,0:T(8,128)} %get-tuple-element.8) | copy-start | bytes 589828

commit v2 on v1

--- a/solution.py
+++ b/solution.py
@@ -15,6 +15,8 @@
 LANES = 128
 MESH = pl.DeviceIdType.MESH
 VMEM_BYTES = 56 * 2**20
+KEEP_BYTES = 8 * 2**20
+TILE = 16
 F32 = jnp.float32
 BF16 = jnp.bfloat16
 
@@ -45,19 +47,19 @@
 
 
 def exchange_kernel(
-    owners, groups, candidates, tokens,
+    owners, groups, candidates, tokens, keep,
     q_ref, pages_ref, owner_ref, slot_ref,
     loss_ref, qgrad_ref, back_ref, asked_ref,
     q_all, d_round, asked, asked_smem, send, fetched, turned, sums, rows_ref, weight_ref,
-    shares, terms, q_part, q_got,
+    shares, terms, q_part, q_got, kept,
     ask_out, ask_in, page_out, page_in, back_out, back_in,
     q_out, q_in, sum_out, sum_in, part_out, part_in, local_sem,
 ):
+    kept = kept if keep else None
     me = lax.axis_index("pages")
     mine = lax.axis_index("query")
-    page_count = pages_ref.shape[0]
+    page_count, patches, width = pages_ref.shape
     rows = q_ref.shape[0]
-    padded = rows_ref.shape[0]
 
     def to_owner(k):
         return lax.rem(me + k, owners)
@@ -85,6 +87,14 @@
 
     def each(count, body):
         lax.fori_loop(1, count, lambda k, c: (body(k), c)[1], 0)
+
+    def far_first(count, body):
+        def step(i, carry):
+            half = lax.div(i + 1, 2)
+            body(jnp.where(lax.rem(i, 2) == 1, count // 2 + half, count // 2 - half))
+            return carry
+
+        lax.fori_loop(0, count - 1, step, 0)
 
     barrier = pltpu.get_barrier_semaphore()
     each(owners, lambda k: pl.semaphore_signal(
@@ -122,10 +132,12 @@
 
     def serve(k):
         to = to_owner(k)
-        send[k] = d_round[jnp.maximum(asked_smem[to, 0, me], 0)]
-        across_pages(send.at[k], fetched.at[me], page_out, page_in, k).start()
-
-    each(owners, serve)
+        send[k, :patches] = d_round[jnp.maximum(asked_smem[to, 0, me], 0)]
+        across_pages(
+            send.at[k, pl.ds(0, patches)], fetched.at[me], page_out, page_in, k
+        ).start()
+
+    far_first(owners, serve)
     fetched[me] = d_round[jnp.maximum(asked_smem[me, 0, me], 0)]
 
     def query_arrived(k):
@@ -135,7 +147,9 @@
     each(groups, query_arrived)
 
     def page_arrived(k):
-        across_pages(send.at[k], fetched.at[from_owner(k)], page_out, page_in, k).wait()
+        across_pages(
+            send.at[k, pl.ds(0, patches)], fetched.at[from_owner(k)], page_out, page_in, k
+        ).wait()
 
     each(owners, page_arrived)
 
@@ -149,9 +163,10 @@
         page = fetched[owner_ref[0, c]]
         turned[c] = page.T
         for g in range(groups):
-            sums[mine, c, :, g * rows : (g + 1) * rows] = jnp.sum(
-                exponentials(page, g), axis=0, keepdims=True
-            )
+            powers = exponentials(page, g)
+            if kept is not None:
+                kept[c, g] = powers
+            sums[mine, c, :, g * rows : (g + 1) * rows] = jnp.sum(powers, axis=0, keepdims=True)
         return carry
 
     lax.fori_loop(0, candidates, forward, 0)
@@ -177,8 +192,13 @@
     losses = jnp.log(denominator) - logits[0:1]
     positive = jnp.where(which == 0, 1.0, 0.0)
     weights = (LOSS_SCALE * INV_TEMP / tokens) * (powers / denominator - positive) / totals
-    for g in range(groups):
-        loss_ref[g] = losses[:, g * rows : (g + 1) * rows]
+    own = losses[:, :rows]
+    for g in range(1, groups):
+        own = jnp.where(mine == g, losses[:, g * rows : (g + 1) * rows], own)
+    place = lax.broadcasted_iota(jnp.int32, (LANES, rows), 0)
+    token = lax.broadcasted_iota(jnp.int32, (LANES, rows), 1)
+    picked = jnp.sum(jnp.where(token == place * tokens, own, 0.0), axis=1, keepdims=True)
+    loss_ref[...] = jnp.broadcast_to(picked, (LANES, LANES)).T[:1, : rows // tokens]
     for c in range(candidates):
         weight_ref[c] = weights[c : c + 1]
 
@@ -186,12 +206,17 @@
         page = fetched[owner_ref[0, c]]
         term = jnp.zeros(page.shape, F32)
         for g in range(groups):
-            share = (
-                weight_ref[c, :, g * rows : (g + 1) * rows] * exponentials(page, g)
-            ).astype(BF16)
+            powers = exponentials(page, g) if kept is None else kept[c, g]
+            share = (weight_ref[c, :, g * rows : (g + 1) * rows] * powers).astype(BF16)
             shares[c, g] = share
             term = term + jnp.dot(share, q_all[g], preferred_element_type=F32)
-        terms[c] = term.astype(BF16)
+        values = page.astype(F32)
+        along = jnp.sum(values * term, axis=-1, keepdims=True).astype(BF16).astype(F32)
+        terms[c, :patches] = (term - values * along).astype(BF16)
+        flat = jnp.broadcast_to(along, term.shape).T
+        pieces = [flat[:1, i : i + width] for i in range(0, patches, width)]
+        pieces.append(jnp.zeros((TILE - len(pieces), width), F32))
+        terms[c, patches:] = jnp.concatenate(pieces, axis=0).astype(BF16)
         return carry
 
     lax.fori_loop(0, candidates, backward, 0)
@@ -206,7 +231,7 @@
         send[k] = term_for(to_owner(k))
         across_pages(send.at[k], back_ref.at[me], back_out, back_in, k).start()
 
-    each(owners, give_back)
+    far_first(owners, give_back)
     back_ref[me] = term_for(me)
 
     for k in range(1, groups + 1):
@@ -234,35 +259,40 @@
     each(owners, back_arrived)
 
 
-def page_kernel(owners, asked_ref, pages_ref, back_ref, out_ref, total):
+def finish_kernel(
+    owners, asked_ref, pages_ref, back_ref, q_in_ref, loss_in_ref, loss_ref, q_out_ref, out_ref
+):
     me = lax.axis_index("pages")
-    here = pages_ref.shape[0]
-    for i in range(here):
-        page = pl.program_id(0) * here + i
-
-        def count(r, found):
-            return found + jnp.where(asked_ref[r, me] == page, 1, 0)
-
-        found = lax.fori_loop(0, owners, count, jnp.int32(0))
-
-        @pl.when(found == 0)
+    page_count, patches, width = pages_ref.shape
+    loss_ref[...] = loss_in_ref[...]
+    q_out_ref[...] = q_in_ref[...]
+
+    def clear(j, carry):
+        out_ref[j] = jnp.zeros((patches, width), F32)
+        return carry
+
+    lax.fori_loop(0, page_count, clear, 0)
+
+    def add(r, carry):
+        slot = asked_ref[r, 0, me]
+
+        @pl.when(slot >= 0)
         def _():
-            out_ref[i] = jnp.zeros(out_ref.shape[1:], F32)
-
-        @pl.when(found > 0)
-        def _():
-            total[...] = jnp.zeros_like(total)
-
-            def add(r, carry):
-                @pl.when(asked_ref[r, me] == page)
-                def _():
-                    total[...] += back_ref[r].astype(F32)
-
-                return carry
-
-            lax.fori_loop(0, owners, add, 0)
-            d_unit, d_inv = normalize(pages_ref[i])
-            out_ref[i] = unnormalize_grad(d_unit, d_inv, total[...])
+            d_unit, d_inv = normalize(pages_ref[slot])
+            flat = back_ref[r, patches:].astype(F32)
+            along = jnp.concatenate(
+                [
+                    jnp.broadcast_to(flat[i : i + 1], (width, width)).T
+                    for i in range(patches // width)
+                ],
+                axis=0,
+            )
+            term = back_ref[r, :patches].astype(F32) + along * d_unit.astype(BF16).astype(F32)
+            out_ref[slot] += unnormalize_grad(d_unit, d_inv, term)
+
+        return carry
+
+    lax.fori_loop(0, owners, add, 0)
 
 
 def local(queries, pages, cand_owner, cand_slot):
@@ -274,15 +304,19 @@
     rows = queries_local * tokens
     everyone = groups * rows
     padded = -(-candidates // 8) * 8
+    assert queries_local <= LANES and owners <= LANES
+    assert patches % width == 0 and patches // width < TILE and tokens & (tokens - 1) == 0
+    grid = (candidates, groups, patches, rows)
+    keep = 4 * math.prod(grid) <= KEEP_BYTES
     dma = pltpu.SemaphoreType.DMA
     vmem = pl.BlockSpec(memory_space=pltpu.VMEM)
     smem = pl.BlockSpec(memory_space=pltpu.SMEM)
     losses, query_grad, back, asked = pl.pallas_call(
-        functools.partial(exchange_kernel, owners, groups, candidates, tokens),
+        functools.partial(exchange_kernel, owners, groups, candidates, tokens, keep),
         out_shape=(
-            jax.ShapeDtypeStruct((groups, 1, rows), F32),
+            jax.ShapeDtypeStruct((1, queries_local), F32),
             jax.ShapeDtypeStruct((rows, width), F32),
-            jax.ShapeDtypeStruct((owners, patches, width), BF16),
+            jax.ShapeDtypeStruct((owners, patches + TILE, width), BF16),
             jax.ShapeDtypeStruct((owners, 1, LANES), jnp.int32),
         ),
         in_specs=[vmem, vmem, smem, smem],
@@ -292,16 +326,17 @@
             pltpu.VMEM((page_count, patches, width), BF16),
             pltpu.VMEM((owners, 1, LANES), jnp.int32),
             pltpu.SMEM((owners, 1, LANES), jnp.int32),
-            pltpu.VMEM((owners, patches, width), BF16),
+            pltpu.VMEM((owners, patches + TILE, width), BF16),
             pltpu.VMEM((owners, patches, width), BF16),
             pltpu.VMEM((candidates, width, patches), BF16),
             pltpu.VMEM((groups, candidates, 1, everyone), F32),
             pltpu.VMEM((padded, everyone), F32),
             pltpu.VMEM((candidates, 1, everyone), F32),
-            pltpu.VMEM((candidates, groups, patches, rows), BF16),
-            pltpu.VMEM((candidates, patches, width), BF16),
+            pltpu.VMEM(grid, BF16),
+            pltpu.VMEM((candidates, patches + TILE, width), BF16),
             pltpu.VMEM((groups, width, rows), F32),
             pltpu.VMEM((groups, width, rows), F32),
+            pltpu.VMEM(grid if keep else (8, LANES), F32),
         ]
         + [dma((owners,))] * 6
         + [dma((groups,))] * 6
@@ -311,24 +346,19 @@
         ),
     )(queries.reshape(rows, width), pages, cand_owner, cand_slot)
 
-    block = max(1, page_count // 4)
-    whole = pl.BlockSpec((owners, patches, width), lambda i, asked: (0, 0, 0))
-    some = pl.BlockSpec((block, patches, width), lambda i, asked: (i, 0, 0))
-    page_grad = pl.pallas_call(
-        functools.partial(page_kernel, owners),
-        out_shape=jax.ShapeDtypeStruct((page_count, patches, width), F32),
-        grid_spec=pltpu.PrefetchScalarGridSpec(
-            num_scalar_prefetch=1,
-            grid=(page_count // block,),
-            in_specs=[some, whole],
-            out_specs=some,
-            scratch_shapes=[pltpu.VMEM((patches, width), F32)],
+    losses, query_grad, page_grad = pl.pallas_call(
+        functools.partial(finish_kernel, owners),
+        out_shape=(
+            jax.ShapeDtypeStruct(losses.shape, F32),
+            jax.ShapeDtypeStruct(query_grad.shape, F32),
+            jax.ShapeDtypeStruct((page_count, patches, width), F32),
         ),
+        in_specs=[smem, vmem, vmem, vmem, vmem],
+        out_specs=(vmem, vmem, vmem),
         compiler_params=pltpu.CompilerParams(vmem_limit_bytes=VMEM_BYTES),
-    )(asked.reshape(owners, LANES), pages, back)
-    own = lax.dynamic_index_in_dim(losses, lax.axis_index("query"), 0, keepdims=False)
+    )(asked, pages, back, query_grad, losses)
     return (
-        own.reshape(queries_local, tokens)[:, 0][None],
+        losses,
         query_grad.reshape(1, queries_local, tokens, width),
         page_grad,
     )

time: 50.8 us -> 47.9 us (0.943)
  the two profiles are of different devices: /device:TPU:26 before, /device:TPU:0 now
where the time goes in v2:
time: 47.9 us; the launch traced here: 47.3 us
  Pallas kernels  46.7 us (97%)
  between operations  0.64 us (1%)
    pallas_call x1, Pallas kernels, local(): pl.pallas_call(functools.partial(exchange_kernel, owners, groups, candida...  43.3 us
    pallas_call x1, Pallas kernels, local(): pl.pallas_call(functools.partial(finish_kernel, owners), out_shape=(jax.S...  3.36 us

profile of v2, /device:TPU:0, one launch (start us, length us, event | category | flops | bytes accessed | tf_op | source)
XLA Modules:
  0.0 47.3 jit_solution(15728437447081402652)
XLA Ops:
  0.6 43.3 %shard_map.67 = (f32[1,12]{1,0:T(1,128)}, f32[384,128]{1,0:T(8,128)}, bf16[8,272,128]{2,1,0:T(8,128)(2,1)}, s32[8,1,128]{2,1,0:T(1,128)}) custom-call(bf16[384,128]{1,0:T(8,128)(2,1)} %bitcast.2, bf16[16,256,128]{2,1,0:T(8,128)(2,1)} %pages_ref.3, s32[1,3]{1,0:T(1,128)} %owner_ref.1, s32[1,3]{1,0:T(1,128)} %slot_ref.1), custom_call_target="tpu_custom_call" | custom-call | tf_op jit(solution)/shard_map/pallas_call | solution.py:314
  44.0 3.4 %shard_map.68 = (f32[1,12]{1,0:T(1,128)}, f32[384,128]{1,0:T(8,128)}, f32[16,256,128]{2,1,0:T(8,128)}) custom-call(s32[8,1,128]{2,1,0:T(1,128)} %get-tuple-element.10.asked_ref, bf16[16,256,128]{2,1,0:T(8,128)(2,1)} %pages_ref.3, bf16[8,272,128]{2,1,0:T(8,128)(2,1)} %get-tuple-element.11.back_ref, f32[384,128]{1,0:T(8,128)} %get-tuple-element.12.q_in_ref, ...), custom_call_target="tpu_custom_call" | custom-call | tf_op jit(solution)/shard_map/pallas_call | solution.py:349

commit v3 on v2

--- a/solution.py
+++ b/solution.py
@@ -88,14 +88,6 @@
     def each(count, body):
         lax.fori_loop(1, count, lambda k, c: (body(k), c)[1], 0)
 
-    def far_first(count, body):
-        def step(i, carry):
-            half = lax.div(i + 1, 2)
-            body(jnp.where(lax.rem(i, 2) == 1, count // 2 + half, count // 2 - half))
-            return carry
-
-        lax.fori_loop(0, count - 1, step, 0)
-
     barrier = pltpu.get_barrier_semaphore()
     each(owners, lambda k: pl.semaphore_signal(
         barrier, inc=1, device_id=(to_owner(k), mine), device_id_type=MESH))
@@ -137,7 +129,7 @@
             send.at[k, pl.ds(0, patches)], fetched.at[me], page_out, page_in, k
         ).start()
 
-    far_first(owners, serve)
+    each(owners, serve)
     fetched[me] = d_round[jnp.maximum(asked_smem[me, 0, me], 0)]
 
     def query_arrived(k):
@@ -231,7 +223,7 @@
         send[k] = term_for(to_owner(k))
         across_pages(send.at[k], back_ref.at[me], back_out, back_in, k).start()
 
-    far_first(owners, give_back)
+    each(owners, give_back)
     back_ref[me] = term_for(me)
 
     for k in range(1, groups + 1):
@@ -240,16 +232,19 @@
         def query_side(c, total, g=g):
             return total + jnp.dot(turned[c], shares[c, g], preferred_element_type=F32)
 
-        q_part[k - 1] = lax.fori_loop(
-            0, candidates, query_side, jnp.zeros(q_part.shape[1:], F32)
-        )
+        part = lax.fori_loop(0, candidates, query_side, jnp.zeros((width, rows), F32))
+        across = q_all[g].T.astype(F32)
         if k < groups:
+            along = jnp.sum(across * part, axis=0, keepdims=True).astype(BF16).astype(F32)
+            q_part[k - 1, :width] = (part - across * along).astype(BF16)
+            q_part[k - 1, width:] = jnp.broadcast_to(along, (TILE, rows)).astype(BF16)
             across_query(q_part.at[k - 1], q_got.at[k - 1], part_out, part_in, k).start()
 
-    total = q_part[groups - 1]
+    total = part
     for k in range(1, groups):
         across_query(q_part.at[k - 1], q_got.at[k - 1], part_out, part_in, k).wait()
-        total = total + q_got[k - 1]
+        got = q_got[k - 1].astype(F32)
+        total = total + (got[:width] + across * got[width : width + 1])
     q_unit, q_inv = normalize(q_ref[...])
     qgrad_ref[...] = unnormalize_grad(q_unit, q_inv, total.T)
 
@@ -334,8 +329,8 @@
             pltpu.VMEM((candidates, 1, everyone), F32),
             pltpu.VMEM(grid, BF16),
             pltpu.VMEM((candidates, patches + TILE, width), BF16),
-            pltpu.VMEM((groups, width, rows), F32),
-            pltpu.VMEM((groups, width, rows), F32),
+            pltpu.VMEM((groups, width + TILE, rows), BF16),
+            pltpu.VMEM((groups, width + TILE, rows), BF16),
             pltpu.VMEM(grid if keep else (8, LANES), F32),
         ]
         + [dma((owners,))] * 6

time: 47.9 us -> 47.7 us (level)
  the two profiles are of different devices: /device:TPU:0 before, /device:TPU:26 now
where the time goes in v3:
time: 47.7 us; the launch traced here: 47.5 us
  Pallas kernels  46.9 us (98%)
  between operations  0.64 us (1%)
    pallas_call x1, Pallas kernels, local(): pl.pallas_call(functools.partial(exchange_kernel, owners, groups, candida...  42.5 us
    pallas_call x1, Pallas kernels, local(): pl.pallas_call(functools.partial(finish_kernel, owners), out_shape=(jax.S...  4.35 us

profile of v3, /device:TPU:26, one launch (start us, length us, event | category | flops | bytes accessed | tf_op | source)
XLA Modules:
  0.0 47.5 jit_solution(12517855287954799901)
XLA Ops:
  0.6 42.5 %shard_map.67 = (f32[1,12]{1,0:T(1,128)}, f32[384,128]{1,0:T(8,128)}, bf16[8,272,128]{2,1,0:T(8,128)(2,1)}, s32[8,1,128]{2,1,0:T(1,128)}) custom-call(bf16[384,128]{1,0:T(8,128)(2,1)} %bitcast.2, bf16[16,256,128]{2,1,0:T(8,128)(2,1)} %pages_ref.3, s32[1,3]{1,0:T(1,128)} %owner_ref.1, s32[1,3]{1,0:T(1,128)} %slot_ref.1), custom_call_target="tpu_custom_call" | custom-call | tf_op jit(solution)/shard_map/pallas_call | solution.py:309
  43.2 4.4 %shard_map.68 = (f32[1,12]{1,0:T(1,128)}, f32[384,128]{1,0:T(8,128)}, f32[16,256,128]{2,1,0:T(8,128)}) custom-call(s32[8,1,128]{2,1,0:T(1,128)} %get-tuple-element.10.asked_ref, bf16[16,256,128]{2,1,0:T(8,128)(2,1)} %pages_ref.3, bf16[8,272,128]{2,1,0:T(8,128)(2,1)} %get-tuple-element.11.back_ref, f32[384,128]{1,0:T(8,128)} %get-tuple-element.12.q_in_ref, ...), custom_call_target="tpu_custom_call" | custom-call | tf_op jit(solution)/shard_map/pallas_call | solution.py:344

commit v4 on v3

--- a/solution.py
+++ b/solution.py
@@ -161,7 +161,7 @@
             sums[mine, c, :, g * rows : (g + 1) * rows] = jnp.sum(powers, axis=0, keepdims=True)
         return carry
 
-    lax.fori_loop(0, candidates, forward, 0)
+    lax.fori_loop(0, candidates, forward, 0, unroll=candidates <= 4)
     each(groups, lambda k: across_query(sums.at[mine], sums.at[mine], sum_out, sum_in, k).start())
 
     def sums_arrived(k):
@@ -211,7 +211,7 @@
         terms[c, patches:] = jnp.concatenate(pieces, axis=0).astype(BF16)
         return carry
 
-    lax.fori_loop(0, candidates, backward, 0)
+    lax.fori_loop(0, candidates, backward, 0, unroll=candidates <= 4)
 
     def term_for(owner):
         place = jnp.int32(0)
@@ -232,7 +232,7 @@
         def query_side(c, total, g=g):
             return total + jnp.dot(turned[c], shares[c, g], preferred_element_type=F32)
 
-        part = lax.fori_loop(0, candidates, query_side, jnp.zeros((width, rows), F32))
+        part = lax.fori_loop(0, candidates, query_side, jnp.zeros((width, rows), F32), unroll=candidates <= 4)
         across = q_all[g].T.astype(F32)
         if k < groups:
             along = jnp.sum(across * part, axis=0, keepdims=True).astype(BF16).astype(F32)

time: 47.7 us -> 46 us (0.964)
  Pallas kernels: 46.9 us -> 45.1 us
    pallas_call x1, Pallas kernels: 42.5 us -> 41.5 us  [local(): pl.pallas_call(functools.partial(exchange_kernel, owners, groups, candida...]
    pallas_call x1, Pallas kernels: 4.35 us -> 3.61 us  [local(): pl.pallas_call(functools.partial(finish_kernel, owners), out_shape=(jax.S...]
where the time goes in v4:
time: 46 us; the launch traced here: 45.7 us
  Pallas kernels  45.1 us (98%)
  between operations  0.64 us (1%)
    pallas_call x1, Pallas kernels, local(): pl.pallas_call(functools.partial(exchange_kernel, owners, groups, candida...  41.5 us
    pallas_call x1, Pallas kernels, local(): pl.pallas_call(functools.partial(finish_kernel, owners), out_shape=(jax.S...  3.61 us

profile of v4, /device:TPU:26, one launch (start us, length us, event | category | flops | bytes accessed | tf_op | source)
XLA Modules:
  0.0 45.7 jit_solution(12432453124269762217)
XLA Ops:
  0.6 41.5 %shard_map.67 = (f32[1,12]{1,0:T(1,128)}, f32[384,128]{1,0:T(8,128)}, bf16[8,272,128]{2,1,0:T(8,128)(2,1)}, s32[8,1,128]{2,1,0:T(1,128)}) custom-call(bf16[384,128]{1,0:T(8,128)(2,1)} %bitcast.2, bf16[16,256,128]{2,1,0:T(8,128)(2,1)} %pages_ref.3, s32[1,3]{1,0:T(1,128)} %owner_ref.1, s32[1,3]{1,0:T(1,128)} %slot_ref.1), custom_call_target="tpu_custom_call" | custom-call | tf_op jit(solution)/shard_map/pallas_call | solution.py:309
  42.1 3.6 %shard_map.68 = (f32[1,12]{1,0:T(1,128)}, f32[384,128]{1,0:T(8,128)}, f32[16,256,128]{2,1,0:T(8,128)}) custom-call(s32[8,1,128]{2,1,0:T(1,128)} %get-tuple-element.10.asked_ref, bf16[16,256,128]{2,1,0:T(8,128)(2,1)} %pages_ref.3, bf16[8,272,128]{2,1,0:T(8,128)(2,1)} %get-tuple-element.11.back_ref, f32[384,128]{1,0:T(8,128)} %get-tuple-element.12.q_in_ref, ...), custom_call_target="tpu_custom_call" | custom-call | tf_op jit(solution)/shard_map/pallas_call | solution.py:344
